TPU v7x, 32 devices: a whole 2x2x4 slice. The times are simulated.
32 devices in a mesh: group: 2 (over x), gx: 8 (over z, y), gy: 2 (over core).
Axes of the slice: x: 2, y: 2, z: 4, core: 2. Of those that a mesh axis runs over, the one named last changes fastest.
Arguments:
- body_force: float32 [3, 32, 64, 512], P(None, ('group', 'gx'), 'gy'), parts along dimension 1, may hold values from -20 to 20
- phase_label: int32 [32, 64, 512], P(('group', 'gx'), 'gy'), parts along dimension 0, may hold values from 0 to 1
- grain_modulus: float32 [32, 64, 512], P(('group', 'gx'), 'gy'), parts along dimension 0, may hold values from 0.5 to 2
Outputs:
- displacement: float32 [3, 32, 64, 512], P(None, ('group', 'gx'), 'gy'), parts along dimension 1
- sensitivity: float32 [32, 64, 512], P(('group', 'gx'), 'gy'), parts along dimension 0
There are 2 independent parts, one for each index of `group`. A program takes and returns all parts, laid end to end along the dimension named above; each array names one. Nothing has to cross between parts.
All inputs are finite; a program needn't handle non-finite values.
Results may differ from a plain program's by a relative error of at most 0.0002.
Values sent between devices are 32-bit elements; how exact they have to be, the bound alone decides.
A program may use at most 64 MiB of HBM per device.

v0:
```python
import math

import jax
import jax.numpy as jnp
import numpy as np
from jax import lax
from jax.sharding import PartitionSpec as P

ITERS = 3


pore_modulus = 0.05


def passed_along(value, axis, steps):
    count = lax.axis_size(axis)
    pairs = [(source, (source + steps) % count) for source in range(count)]
    return lax.ppermute(value, axis, pairs)


def element_matrix():
    poisson = 0.3
    lame = poisson / ((1.0 + poisson) * (1.0 - 2.0 * poisson))
    shear = 0.5 / (1.0 + poisson)
    elastic = np.zeros((6, 6))
    elastic[:3, :3] = lame
    for index in range(3):
        elastic[index, index] += 2.0 * shear
        elastic[index + 3, index + 3] = shear
    gauss = [0.5 - 0.5 / math.sqrt(3.0), 0.5 + 0.5 / math.sqrt(3.0)]
    matrix = np.zeros((24, 24))
    for point_x in gauss:
        for point_y in gauss:
            for point_z in gauss:
                strain = np.zeros((6, 24))
                corner = 0
                for side_x in (0, 1):
                    for side_y in (0, 1):
                        for side_z in (0, 1):
                            weight_x = point_x if side_x else 1.0 - point_x
                            weight_y = point_y if side_y else 1.0 - point_y
                            weight_z = point_z if side_z else 1.0 - point_z
                            slope_x = (2 * side_x - 1) * weight_y * weight_z
                            slope_y = (2 * side_y - 1) * weight_x * weight_z
                            slope_z = (2 * side_z - 1) * weight_x * weight_y
                            column = 3 * corner
                            strain[0, column] = slope_x
                            strain[1, column + 1] = slope_y
                            strain[2, column + 2] = slope_z
                            strain[3, column] = slope_y
                            strain[3, column + 1] = slope_x
                            strain[4, column + 1] = slope_z
                            strain[4, column + 2] = slope_y
                            strain[5, column] = slope_z
                            strain[5, column + 2] = slope_x
                            corner += 1
                matrix += strain.T @ elastic @ strain / 8.0
    return matrix.astype(np.float32)


def take_corners(extended, offset, x_count, y_count):
    gathered = []
    for side_x in (0, 1):
        for side_y in (0, 1):
            for side_z in (0, 1):
                view = extended[
                    :,
                    offset + side_x : offset + side_x + x_count,
                    offset + side_y : offset + side_y + y_count,
                ]
                if side_z == 0:
                    view = jnp.concatenate([jnp.zeros_like(view[..., :1]), view[..., :-1]], 3)
                gathered.append(view)
    return jnp.stack(gathered, 0).reshape(24, -1)


def spread_forces(values, x_count, y_count, z_count):
    blocks = values.reshape(8, 3, x_count, y_count, z_count)
    summed = jnp.zeros((3, x_count + 1, y_count + 1, z_count), jnp.float32)
    corner = 0
    for side_x in (0, 1):
        for side_y in (0, 1):
            for side_z in (0, 1):
                block = blocks[corner]
                if side_z == 0:
                    block = jnp.concatenate([block[..., 1:], jnp.zeros_like(block[..., :1])], 3)
                summed = summed + jnp.pad(
                    block, ((0, 0), (side_x, 1 - side_x), (side_y, 1 - side_y), (0, 0))
                )
                corner += 1
    return summed


def element_forces(stiffness, corners, moduli):
    nodal = jnp.dot(
        stiffness, corners, precision=lax.Precision.HIGHEST, preferred_element_type=jnp.float32
    )
    return nodal * moduli[None]


def inner_sum(first, second):
    return lax.psum(jnp.sum(first * second), ("gx", "gy"))


def per_device(body_force, phase_label, grain_modulus):
    x_cells, y_cells, z_cells = phase_label.shape
    moduli = jnp.where(phase_label == 1, grain_modulus, jnp.float32(pore_modulus))
    stiffness = jnp.asarray(element_matrix(), dtype=jnp.float32)
    entries = jnp.diagonal(stiffness)
    flat_moduli = moduli.reshape(-1)

    def node_rims(field):
        x_face = passed_along(field[:, :1], "gx", -1)
        extended = jnp.concatenate([field, x_face], 1)
        y_face = passed_along(extended[:, :, :1], "gy", -1)
        return jnp.concatenate([extended, y_face], 2)

    def fold_rims(summed):
        x_face = passed_along(summed[:, x_cells:], "gx", 1)
        summed = jnp.concatenate([summed[:, :1] + x_face, summed[:, 1:x_cells]], 1)
        y_face = passed_along(summed[:, :, y_cells:], "gy", 1)
        return jnp.concatenate([summed[:, :, :1] + y_face, summed[:, :, 1:y_cells]], 2)

    diagonal = fold_rims(
        spread_forces(entries[:, None] * flat_moduli[None], x_cells, y_cells, z_cells)
    )
    inverse = 1.0 / diagonal
    displacement = jnp.zeros_like(body_force)
    residual = body_force
    precond = inverse * residual
    direction = precond
    norm_now = inner_sum(residual, precond)
    for step in range(ITERS):
        apply_corners = take_corners(node_rims(direction), 0, x_cells, y_cells)
        image = fold_rims(
            spread_forces(
                element_forces(stiffness, apply_corners, flat_moduli), x_cells, y_cells, z_cells
            )
        )
        step_size = norm_now / lax.psum(jnp.sum(direction * image), ("gx", "gy"))
        displacement = displacement + step_size * direction
        residual = residual - step_size * image
        if step + 1 < ITERS:
            precond = inverse * residual
            norm_next = inner_sum(residual, precond)
            direction = precond + norm_next / norm_now * direction
            norm_now = norm_next
    corners = take_corners(node_rims(displacement), 0, x_cells, y_cells)
    nodal = element_forces(stiffness, corners, flat_moduli)
    energy = jnp.sum(corners * nodal, axis=0).reshape(x_cells, y_cells, z_cells)
    return (displacement, -energy)


def solution(mesh):
    in_specs = (
        P(None, ("group", "gx"), "gy", None),
        P(("group", "gx"), "gy", None),
        P(("group", "gx"), "gy", None),
    )
    out_specs = (P(None, ("group", "gx"), "gy", None), P(("group", "gx"), "gy", None))
    return jax.shard_map(
        per_device, mesh=mesh, in_specs=in_specs, out_specs=out_specs, check_vma=False
    )
```

profile of v0, /device:TPU:0, one launch (start us, length us, event | category | flops | bytes accessed | tf_op | source)
XLA Modules:
  0.0 326.0 jit_solution(10578394677607304965)
XLA Ops:
  0.6 1.0 compare_select_fusion
  1.7 1.5 gather_fusion
  6.5 3.0 collective-permute-start
  9.5 9.0 %collective-permute-done = f32[3,1,33,512]{3,2,1,0:T(8,128)S(1)} collective-permute-done((f32[3,1,33,512]{3,2,1,0:T(8,128)S(1)}, f32[3,1,33,512]{3,2,1,0:T(8,128)S(1)}, u32[]{:S(2)}, u32[]{:S(2)}) %collective-permute-start) | collective-permute-done | bytes 202784 | tf_op jit(solution)/shard_map/ppermute | solution.py:18
  18.6 1.2 collective-permute-done.1
  19.9 1.8 collective-permute-start.2
  21.7 5.2 %collective-permute-done.2 = f32[3,1,32,512]{3,2,1,0:T(8,128)S(1)} collective-permute-done((f32[3,1,32,512]{3,2,1,0:T(8,128)S(1)}, f32[3,1,32,512]{3,2,1,0:T(8,128)S(1)}, u32[]{:S(2)}, u32[]{:S(2)}) %collective-permute-start.2) | collective-permute-done | bytes 196640 | tf_op jit(solution)/shard_map/ppermute | solution.py:18
  27.1 0.9 bitcast_dynamic-update-slice_fusion.19
  30.8 0.9 bitcast_dynamic-update-slice_fusion.16
  34.3 4.6 %reshape.88 = f32[24,32768]{1,0:T(8,128)} reshape(f32[8,3,2,32,512]{4,3,2,1,0:T(8,128)} %fusion.39) | data formatting | bytes 6291456 | tf_op jit(solution)/shard_map/reshape | solution.py:74
  38.9 4.8 %fusion.4 = f32[24,32768]{1,0:T(8,128)S(1)} fusion(f32[24,32768]{1,0:T(8,128)} %reshape.88, f32[24,24]{1,0:T(8,128)S(1)} %copy-done, f32[32768]{0:T(1024)S(1)} %bitcast.217), kind=kOutput, calls=%fused_computation.9 | convolution fusion | flops 227278848 | bytes 6424832 | tf_op jit(solution)/shard_map/dot_general | solution.py:95
  46.7 11.0 %collective-permute-done.4 = f32[3,1,33,512]{3,2,1,0:T(8,128)S(1)} collective-permute-done((f32[3,1,33,512]{3,2,1,0:T(8,128)S(1)}, f32[3,1,33,512]{3,2,1,0:T(8,128)S(1)}, u32[]{:S(2)}, u32[]{:S(2)}) %collective-permute-start.4) | collective-permute-done | bytes 202784 | tf_op jit(solution)/shard_map/ppermute | solution.py:18
  57.9 1.2 collective-permute-done.5
  59.9 31.6 %all-reduce.64 = (f32[]{:T(128)}, f32[]{:T(128)}) all-reduce(f32[]{:T(128)} %get-tuple-element.3, f32[]{:T(128)} %get-tuple-element.2), channel_id=1, replica_groups=mesh['group'=2,'gx'=8,'gy'=2] {'gx','gy'}, use_global_device_ids=true, to_apply=%region_1.2 | all-reduce | flops 2 | bytes 16 | tf_op jit(solution)/shard_map/psum | solution.py:102
  93.6 30.1 %psum.44 = f32[]{:T(128)} all-reduce(f32[]{:T(128)} %get-tuple-element.6), channel_id=1, replica_groups=mesh['group'=2,'gx'=8,'gy'=2] {'gx','gy'}, use_global_device_ids=true, to_apply=%region_5.6 | all-reduce | flops 1 | bytes 8 | tf_op jit(solution)/shard_map/psum | solution.py:102
  125.5 6.7 %collective-permute-done.6 = f32[3,1,32,512]{3,2,1,0:T(8,128)S(1)} collective-permute-done((f32[3,1,32,512]{3,2,1,0:T(8,128)S(1)}, f32[3,1,32,512]{3,2,1,0:T(8,128)S(1)}, u32[]{:S(2)}, u32[]{:S(2)}) %collective-permute-start.6) | collective-permute-done | bytes 196640 | tf_op jit(solution)/shard_map/ppermute | solution.py:18
  135.9 0.9 bitcast_dynamic-update-slice_fusion.11
  139.4 4.6 %reshape.89 = f32[24,32768]{1,0:T(8,128)} reshape(f32[8,3,2,32,512]{4,3,2,1,0:T(8,128)} %fusion.34) | data formatting | bytes 6291456 | tf_op jit(solution)/shard_map/reshape | solution.py:74
  144.0 4.8 %fusion.3 = f32[24,32768]{1,0:T(8,128)S(1)} fusion(f32[24,32768]{1,0:T(8,128)} %reshape.89, f32[24,24]{1,0:T(8,128)S(1)} %copy-done, f32[32768]{0:T(1024)S(1)} %bitcast.218), kind=kOutput, calls=%fused_computation.7 | convolution fusion | flops 227278848 | bytes 6424832 | tf_op jit(solution)/shard_map/dot_general | solution.py:95
  151.8 11.0 %collective-permute-done.8 = f32[3,1,33,512]{3,2,1,0:T(8,128)S(1)} collective-permute-done((f32[3,1,33,512]{3,2,1,0:T(8,128)S(1)}, f32[3,1,33,512]{3,2,1,0:T(8,128)S(1)}, u32[]{:S(2)}, u32[]{:S(2)}) %collective-permute-start.8) | collective-permute-done | bytes 202784 | tf_op jit(solution)/shard_map/ppermute | solution.py:18
  163.0 1.2 collective-permute-done.9
  164.9 30.3 %psum.45 = f32[]{:T(128)} all-reduce(f32[]{:T(128)} %multiply_reduce_fusion.1), channel_id=1, replica_groups=mesh['group'=2,'gx'=8,'gy'=2] {'gx','gy'}, use_global_device_ids=true, to_apply=%region_7.8 | all-reduce | flops 1 | bytes 8 | tf_op jit(solution)/shard_map/psum | solution.py:140
  197.2 30.1 %psum.46 = f32[]{:T(128)} all-reduce(f32[]{:T(128)} %multiply_reduce_fusion), channel_id=1, replica_groups=mesh['group'=2,'gx'=8,'gy'=2] {'gx','gy'}, use_global_device_ids=true, to_apply=%region_9.10 | all-reduce | flops 1 | bytes 8 | tf_op jit(solution)/shard_map/psum | solution.py:102
  229.2 6.7 %collective-permute-done.10 = f32[3,1,32,512]{3,2,1,0:T(8,128)S(1)} collective-permute-done((f32[3,1,32,512]{3,2,1,0:T(8,128)S(1)}, f32[3,1,32,512]{3,2,1,0:T(8,128)S(1)}, u32[]{:S(2)}, u32[]{:S(2)}) %collective-permute-start.10) | collective-permute-done | bytes 196640 | tf_op jit(solution)/shard_map/ppermute | solution.py:18
  243.1 4.6 %reshape.90 = f32[24,32768]{1,0:T(8,128)} reshape(f32[8,3,2,32,512]{4,3,2,1,0:T(8,128)} %fusion.29) | data formatting | bytes 6291456 | tf_op jit(solution)/shard_map/reshape | solution.py:74
  247.7 4.8 %fusion.2 = f32[24,32768]{1,0:T(8,128)S(1)} fusion(f32[24,32768]{1,0:T(8,128)} %reshape.90, f32[24,24]{1,0:T(8,128)S(1)} %copy-done, f32[32768]{0:T(1024)S(1)} %bitcast.219), kind=kOutput, calls=%fused_computation.5 | convolution fusion | flops 227278848 | bytes 6424832 | tf_op jit(solution)/shard_map/dot_general | solution.py:95
  255.5 11.0 %collective-permute-done.12 = f32[3,1,33,512]{3,2,1,0:T(8,128)S(1)} collective-permute-done((f32[3,1,33,512]{3,2,1,0:T(8,128)S(1)}, f32[3,1,33,512]{3,2,1,0:T(8,128)S(1)}, u32[]{:S(2)}, u32[]{:S(2)}) %collective-permute-start.12) | collective-permute-done | bytes 202784 | tf_op jit(solution)/shard_map/ppermute | solution.py:18
  266.7 1.2 collective-permute-done.13
  268.6 30.3 %psum.47 = f32[]{:T(128)} all-reduce(f32[]{:T(128)} %fusion.28), channel_id=1, replica_groups=mesh['group'=2,'gx'=8,'gy'=2] {'gx','gy'}, use_global_device_ids=true, to_apply=%region_11.12 | all-reduce | flops 1 | bytes 8 | tf_op jit(solution)/shard_map/psum | solution.py:140
  300.8 6.5 %collective-permute-done.14 = f32[3,1,32,512]{3,2,1,0:T(8,128)S(1)} collective-permute-done((f32[3,1,32,512]{3,2,1,0:T(8,128)S(1)}, f32[3,1,32,512]{3,2,1,0:T(8,128)S(1)}, u32[]{:S(2)}, u32[]{:S(2)}) %collective-permute-start.14) | collective-permute-done | bytes 196640 | tf_op jit(solution)/shard_map/ppermute | solution.py:18
  314.5 4.6 %reshape.91 = f32[24,32768]{1,0:T(8,128)} reshape(f32[8,3,2,32,512]{4,3,2,1,0:T(8,128)} %fusion.22) | data formatting | bytes 6291456 | tf_op jit(solution)/shard_map/reshape | solution.py:74
  319.1 6.1 %fusion.5 = f32[32768]{0:T(1024)S(1)} fusion(f32[24,32768]{1,0:T(8,128)} %reshape.91, f32[32768]{0:T(1024)S(1)} %bitcast.220, f32[24,24]{1,0:T(8,128)S(1)} %copy-done), kind=kOutput, calls=%fused_computation.11 | convolution fusion | flops 228818944 | bytes 3410176 | tf_op jit(solution)/shard_map/dot_general | solution.py:95
  (159 shorter events, 44.4 us)
Async XLA Ops:
  6.0 13.8 %copy-start.2 = (f32[3,2,32,512]{3,2,1,0:T(8,128)S(1)}, f32[3,2,32,512]{3,2,1,0:T(8,128)}, u32[]{:S(2)}) copy-start(f32[3,2,32,512]{3,2,1,0:T(8,128)} %param.4) | copy-start | bytes 1179652
  6.5 12.0 %collective-permute-start = (f32[3,1,33,512]{3,2,1,0:T(8,128)S(1)}, f32[3,1,33,512]{3,2,1,0:T(8,128)S(1)}, u32[]{:S(2)}, u32[]{:S(2)}) collective-permute-start(f32[3,1,33,512]{3,2,1,0:T(8,128)S(1)} %slice.503), channel_id=1, source_target_pairs={{0,2},{2,4},{4,6},{6,8},{8,10},{10,12},{12,14},{14,0},{1,3},{3,5},... | collective-permute-start | bytes 608264 | tf_op jit(solution)/shard_map/ppermute | solution.py:18
  18.5 1.2 collective-permute-start.1
  19.9 7.0 %collective-permute-start.2 = (f32[3,1,32,512]{3,2,1,0:T(8,128)S(1)}, f32[3,1,32,512]{3,2,1,0:T(8,128)S(1)}, u32[]{:S(2)}, u32[]{:S(2)}) collective-permute-start(f32[3,1,32,512]{3,2,1,0:T(8,128)S(1)} %slice.506), channel_id=1, source_target_pairs={{0,14},{2,0},{4,2},{6,4},{8,6},{10,8},{12,10},{14,12},{1,15},{3,1}... | collective-permute-start | bytes 589832 | tf_op jit(solution)/shard_map/ppermute | solution.py:18
  27.0 1.9 collective-permute-start.3
  34.3 4.6 %copy-start = (f32[24,24]{1,0:T(8,128)S(1)}, f32[24,24]{1,0:T(8,128)}, u32[]{:S(2)}) copy-start(f32[24,24]{1,0:T(8,128)} %constant.18.clone) | copy-start | bytes 6916
  46.7 11.1 %collective-permute-start.4 = (f32[3,1,33,512]{3,2,1,0:T(8,128)S(1)}, f32[3,1,33,512]{3,2,1,0:T(8,128)S(1)}, u32[]{:S(2)}, u32[]{:S(2)}) collective-permute-start(f32[3,1,33,512]{3,2,1,0:T(8,128)S(1)} %slice.526), channel_id=1, source_target_pairs={{0,2},{2,4},{4,6},{6,8},{8,10},{10,12},{12,14},{14,0},{1,3},{3,5},... | collective-permute-start | bytes 608264 | tf_op jit(solution)/shard_map/ppermute | solution.py:18
  57.8 1.2 collective-permute-start.5
  125.2 6.9 %collective-permute-start.6 = (f32[3,1,32,512]{3,2,1,0:T(8,128)S(1)}, f32[3,1,32,512]{3,2,1,0:T(8,128)S(1)}, u32[]{:S(2)}, u32[]{:S(2)}) collective-permute-start(f32[3,1,32,512]{3,2,1,0:T(8,128)S(1)} %slice.529), channel_id=1, source_target_pairs={{0,14},{2,0},{4,2},{6,4},{8,6},{10,8},{12,10},{14,12},{1,15},{3,1}... | collective-permute-start | bytes 589832 | tf_op jit(solution)/shard_map/ppermute | solution.py:18
  132.1 1.9 collective-permute-start.7
  151.7 11.1 %collective-permute-start.8 = (f32[3,1,33,512]{3,2,1,0:T(8,128)S(1)}, f32[3,1,33,512]{3,2,1,0:T(8,128)S(1)}, u32[]{:S(2)}, u32[]{:S(2)}) collective-permute-start(f32[3,1,33,512]{3,2,1,0:T(8,128)S(1)} %slice.549), channel_id=1, source_target_pairs={{0,2},{2,4},{4,6},{6,8},{8,10},{10,12},{12,14},{14,0},{1,3},{3,5},... | collective-permute-start | bytes 608264 | tf_op jit(solution)/shard_map/ppermute | solution.py:18
  162.9 1.2 collective-permute-start.9
  228.9 6.9 %collective-permute-start.10 = (f32[3,1,32,512]{3,2,1,0:T(8,128)S(1)}, f32[3,1,32,512]{3,2,1,0:T(8,128)S(1)}, u32[]{:S(2)}, u32[]{:S(2)}) collective-permute-start(f32[3,1,32,512]{3,2,1,0:T(8,128)S(1)} %slice.552), channel_id=1, source_target_pairs={{0,14},{2,0},{4,2},{6,4},{8,6},{10,8},{12,10},{14,12},{1,15},{3,1}... | collective-permute-start | bytes 589832 | tf_op jit(solution)/shard_map/ppermute | solution.py:18
  235.9 1.9 collective-permute-start.11
  255.5 11.1 %collective-permute-start.12 = (f32[3,1,33,512]{3,2,1,0:T(8,128)S(1)}, f32[3,1,33,512]{3,2,1,0:T(8,128)S(1)}, u32[]{:S(2)}, u32[]{:S(2)}) collective-permute-start(f32[3,1,33,512]{3,2,1,0:T(8,128)S(1)} %slice.572), channel_id=1, source_target_pairs={{0,2},{2,4},{4,6},{6,8},{8,10},{10,12},{12,14},{14,0},{1,3},{3,5},... | collective-permute-start | bytes 608264 | tf_op jit(solution)/shard_map/ppermute | solution.py:18
  266.6 1.2 collective-permute-start.13
  300.4 11.6 %copy-start.1 = (f32[3,2,32,512]{3,2,1,0:T(8,128)}, f32[3,2,32,512]{3,2,1,0:T(8,128)S(1)}, u32[]{:S(2)}) copy-start(f32[3,2,32,512]{3,2,1,0:T(8,128)S(1)} %multiply_add_fusion) | copy-start | bytes 1179652
  300.4 6.8 %collective-permute-start.14 = (f32[3,1,32,512]{3,2,1,0:T(8,128)S(1)}, f32[3,1,32,512]{3,2,1,0:T(8,128)S(1)}, u32[]{:S(2)}, u32[]{:S(2)}) collective-permute-start(f32[3,1,32,512]{3,2,1,0:T(8,128)S(1)} %slice.575), channel_id=1, source_target_pairs={{0,14},{2,0},{4,2},{6,4},{8,6},{10,8},{12,10},{14,12},{1,15},{3,1}... | collective-permute-start | bytes 589832 | tf_op jit(solution)/shard_map/ppermute | solution.py:18
  307.3 1.9 collective-permute-start.15
where the time goes:
time: 327 us; the launch traced here: 326 us
  blocking collectives  152 us (46%)
  waiting for transfers between devices  71.8 us (22%)
  local copies, waits for them, and re-layouts  54.4 us (17%)
  matrix products  20.6 us (6%)
  other arithmetic  12.2 us (4%)
  between operations  8.22 us (3%)
  starting transfers between devices  6.39 us (2%)
    psum x3, blocking collectives, inner_sum(): return lax.psum(jnp.sum(first * second), ('gx', 'gy'))  91.8 us
    ppermute x16, waiting for transfers between devices, passed_along(): return lax.ppermute(value, axis, pairs)  71.8 us
    psum x2, blocking collectives, per_device(): step_size = norm_now / lax.psum(jnp.sum(direction * image), ('gx', 'gy'))  60.5 us
    unnamed x62, local copies, waits for them, and re-layouts  24.5 us
    dot_general x4, matrix products, element_forces(): jnp.dot(stiffness, corners, precision=lax.Precision.HIGHEST, preferred_el...  20.6 us
    reshape x4, local copies, waits for them, and re-layouts, take_corners(): return jnp.stack(gathered, 0).reshape(24, -1)  18.5 us
  transfers between devices with their start and end apart: 16, of which 12 were waited for; matrix products, arithmetic and copies ran while one was open for 2% of the time, Pallas kernels for 0%

commit v1 on v0

v1 whole, which is shorter than its diff:
```python
import functools
import math

import jax
import jax.numpy as jnp
import numpy as np
from jax import lax
from jax.experimental import pallas as pl
from jax.experimental.pallas import tpu as pltpu
from jax.sharding import PartitionSpec as P

PORE = 0.05
SHIFT = 1.0
MESH = pl.DeviceIdType.MESH


def element_matrix():
    poisson = 0.3
    lame = poisson / ((1.0 + poisson) * (1.0 - 2.0 * poisson))
    shear = 0.5 / (1.0 + poisson)
    elastic = np.zeros((6, 6))
    elastic[:3, :3] = lame
    for index in range(3):
        elastic[index, index] += 2.0 * shear
        elastic[index + 3, index + 3] = shear
    gauss = [0.5 - 0.5 / math.sqrt(3.0), 0.5 + 0.5 / math.sqrt(3.0)]
    matrix = np.zeros((24, 24))
    for px in gauss:
        for py in gauss:
            for pz in gauss:
                strain = np.zeros((6, 24))
                corner = 0
                for sx in (0, 1):
                    for sy in (0, 1):
                        for sz in (0, 1):
                            wx = px if sx else 1.0 - px
                            wy = py if sy else 1.0 - py
                            wz = pz if sz else 1.0 - pz
                            dx = (2 * sx - 1) * wy * wz
                            dy = (2 * sy - 1) * wx * wz
                            dz = (2 * sz - 1) * wx * wy
                            col = 3 * corner
                            strain[0, col] = dx
                            strain[1, col + 1] = dy
                            strain[2, col + 2] = dz
                            strain[3, col] = dy
                            strain[3, col + 1] = dx
                            strain[4, col + 1] = dz
                            strain[4, col + 2] = dy
                            strain[5, col] = dz
                            strain[5, col + 2] = dx
                            corner += 1
                matrix += strain.T @ elastic @ strain / 8.0
    return matrix


def mode_matrix():
    pair = np.array([[1.0, 1.0], [-1.0, 1.0]])
    full = np.kron(np.kron(np.kron(pair, pair), pair), np.eye(3))
    return full @ element_matrix() @ full.T / 64.0


K0_DIAGONAL = float(element_matrix()[0, 0])


def constants():
    k = mode_matrix()
    at = lambda mode, comp: 3 * mode + comp
    return dict(
        normal_own=k[at(4, 0), at(4, 0)] - k[at(4, 0), at(2, 1)],
        normal_all=k[at(4, 0), at(2, 1)],
        shear=k[at(2, 0), at(4, 1)],
        pair_own=k[at(6, 0), at(6, 0)],
        pair_other=k[at(6, 0), at(3, 2)],
        triple=k[at(3, 0), at(5, 1)],
        third=k[at(7, 0), at(7, 0)],
    )


K = {name: float(value) for name, value in constants().items()}


def mode_forces(m, modulus):
    g = {}
    own, every = modulus * K["normal_own"], modulus * K["normal_all"]
    keys = [(4, 0), (2, 1), (1, 2)]
    total = every * (m[keys[0]] + m[keys[1]] + m[keys[2]])
    for key in keys:
        g[key] = own * m[key] + total
    shear = modulus * K["shear"]
    for first, second in (((2, 0), (4, 1)), ((1, 1), (2, 2)), ((1, 0), (4, 2))):
        g[first] = g[second] = shear * (m[first] + m[second])
    own, other = modulus * K["pair_own"], modulus * K["pair_other"]
    for first, second in (((6, 0), (3, 2)), ((6, 1), (5, 2)), ((5, 0), (3, 1))):
        g[first] = own * m[first] + other * m[second]
        g[second] = own * m[second] + other * m[first]
    keys = [(3, 0), (5, 1), (6, 2)]
    triple = modulus * K["triple"]
    total = m[keys[0]] + m[keys[1]] + m[keys[2]]
    for key in keys:
        g[key] = triple * (m[key] + total)
    third = modulus * K["third"]
    for comp in range(3):
        g[(7, comp)] = third * m[(7, comp)]
    return g


def mode_energy(m):
    a, b, c = m[(4, 0)], m[(2, 1)], m[(1, 2)]
    total = a + b + c
    energy = K["normal_own"] * (a * a + b * b + c * c) + K["normal_all"] * (total * total)
    squares = None
    for first, second in (((2, 0), (4, 1)), ((1, 1), (2, 2)), ((1, 0), (4, 2))):
        both = m[first] + m[second]
        squares = both * both if squares is None else squares + both * both
    energy = energy + K["shear"] * squares
    squares = cross = None
    for first, second in (((6, 0), (3, 2)), ((6, 1), (5, 2)), ((5, 0), (3, 1))):
        square = m[first] * m[first] + m[second] * m[second]
        product = m[first] * m[second]
        squares = square if squares is None else squares + square
        cross = product if cross is None else cross + product
    energy = energy + K["pair_own"] * squares + (2.0 * K["pair_other"]) * cross
    a, b, c = m[(3, 0)], m[(5, 1)], m[(6, 2)]
    total = a + b + c
    energy = energy + K["triple"] * (a * a + b * b + c * c + total * total)
    a, b, c = m[(7, 0)], m[(7, 1)], m[(7, 2)]
    return energy + K["third"] * (a * a + b * b + c * c)


def kernel(
    n_gx, xc, yc, zc,
    force, label, grain, disp_out, sens_out,
    u0, u1, u2, edge_out, edge_in, mod_own, mod_halo, mod_edge_out, mod_edge_in,
    mod_ext, diag, inv, yz, out, sums, tile, tiles, send_sem, recv_sem, tile_send, tile_recv,
):
    levels = [u0, u1, u2]
    rows = yc + 8
    base = 8
    gx, gy = lax.axis_index("gx"), lax.axis_index("gy")
    other = 1 - gy
    nxt, prv = lax.rem(gx + 1, n_gx), lax.rem(gx + n_gx - 1, n_gx)
    peers = []
    for step in range(n_gx):
        for flip in (0, 1):
            if step or flip:
                peers.append({
                    "gx": lax.rem(gx + step, n_gx) if step else gx,
                    "gy": other if flip else gy,
                })

    barrier = pltpu.get_barrier_semaphore()
    for peer in peers:
        pl.semaphore_signal(barrier, inc=1, device_id=peer, device_id_type=MESH)

    lane = lax.broadcasted_iota(jnp.int32, (1, zc), 1)

    def below(value):
        return jnp.where(lane == 0, 0.0, pltpu.roll(value, 1, 1))

    def above(value):
        return jnp.where(lane == zc - 1, 0.0, pltpu.roll(value, zc - 1, 1))

    sent = []

    def send(src, dst, to_gx, to_gy):
        copy = pltpu.make_async_remote_copy(
            src_ref=src, dst_ref=dst,
            send_sem=send_sem.at[len(sent)], recv_sem=recv_sem.at[len(sent)],
            device_id={"gx": to_gx, "gy": to_gy}, device_id_type=MESH,
        )
        copy.start()
        sent.append(copy)
        return copy

    for x in range(xc):
        values = jnp.where(label[x] == 1, grain[x], jnp.float32(PORE))
        mod_own[x] = values
        mod_edge_out[x, 0:1] = values[yc - 1 : yc]
        mod_ext[x + 1, 1 : yc + 1] = values
    for x in range(xc + 1):
        mod_ext[x, yc + 1 : rows] = jnp.zeros((rows - yc - 1, zc), jnp.float32)
    for u in levels:
        for c in range(3):
            for x in range(xc + 2):
                u[c, x, base + yc : base + yc + 8] = jnp.zeros((8, zc), jnp.float32)
    for x in range(xc):
        mod_edge_out[x, 1:8] = jnp.zeros((7, zc), jnp.float32)
        for level in range(3):
            edge_out[level, x, 6:8] = jnp.zeros((2, zc), jnp.float32)
    sums[...] = jnp.zeros_like(sums)

    pl.semaphore_wait(barrier, len(peers))
    mod_y = send(mod_edge_out, mod_edge_in.at[pl.ds(1, xc)], gx, other)
    mod_x = send(mod_own.at[xc - 1], mod_halo, nxt, gy)
    mod_xy = send(mod_edge_out.at[xc - 1], mod_edge_in.at[0], nxt, other)

    def folded(value):
        total = None
        for r in range(value.shape[0] // 8):
            for l in range(zc // 128):
                part = value[8 * r : 8 * r + 8, 128 * l : 128 * l + 128]
                total = part if total is None else total + part
        return total

    def set_edges(level, x, c, value):
        edge_out[level, x - 1, c : c + 1] = value[0:1]
        edge_out[level, x - 1, 3 + c : 4 + c] = value[yc - 1 : yc]

    own = pl.ds(base, yc)

    def send_y(level):
        return send(edge_out.at[level], edge_in.at[level, pl.ds(1, xc)], gx, other)

    def send_next(level):
        u = levels[level]
        return (
            send(u.at[:, xc, own], u.at[:, 0, own], nxt, gy),
            send(edge_out.at[level, xc - 1], edge_in.at[level, 0], nxt, other),
        )

    def send_prev(level):
        u = levels[level]
        return (
            send(u.at[:, 1, own], u.at[:, xc + 1, own], prv, gy),
            send(edge_out.at[level, 0], edge_in.at[level, xc + 1], prv, other),
        )

    def fill_edges(level, x):
        for c in range(3):
            levels[level][c, x, base + yc : base + yc + 1] = edge_in[level, x, c : c + 1]
            levels[level][c, x, base - 1 : base] = edge_in[level, x, 3 + c : 4 + c]

    def start_plane(x):
        total = mod_ext[x - 1, 0:yc] + mod_ext[x - 1, 1 : yc + 1]
        total = total + mod_ext[x, 0:yc] + mod_ext[x, 1 : yc + 1]
        total = (total + above(total)) * K0_DIAGONAL
        inverse = 1.0 / total
        diag[x - 1] = total
        inv[x - 1] = inverse
        for c in range(3):
            load = force[c, x - 1]
            value = inverse * load
            u0[c, x, base : base + yc] = value
            set_edges(0, x, c, value)
            sums[0] += folded(value * load)

    mod_y.wait_recv()
    for x in range(1, xc + 1):
        mod_ext[x, 0:1] = mod_edge_in[x, 0:1]
    for x in range(xc, 1, -1):
        start_plane(x)
    from_prev = send_next(0)
    mod_x.wait_recv()
    mod_xy.wait_recv()
    mod_ext[0, 0:1] = mod_edge_in[0, 0:1]
    mod_ext[0, 1 : yc + 1] = mod_halo[...]
    start_plane(1)
    from_next = send_prev(0)
    from_y = send_y(0)

    def split_modes(u, x, first, count):
        for c in range(3):
            low = u[c, x, base + first : base + first + count]
            high = u[c, x, base + first + 1 : base + first + 1 + count]
            total, change = high + low, high - low
            low = below(total)
            yz[0, c, x, 0:count] = total + low
            yz[1, c, x, 0:count] = total - low
            low = below(change)
            yz[2, c, x, 0:count] = change + low
            yz[3, c, x, 0:count] = change - low

    def modes_of(cell, r, l):
        m = {}
        for q in range(4):
            for c in range(3):
                low, high = yz[q, c, cell, r, l], yz[q, c, cell + 1, r, l]
                if q:
                    m[(q, c)] = high + low
                m[(4 + q, c)] = high - low
        return m

    lanes = zc // 128

    def apply_cell(cell):
        def body(t, carry):
            r = pl.ds(pl.multiple_of(t // lanes * 8, 8), 8)
            l = pl.ds(pl.multiple_of(lax.rem(t, lanes) * 128, 128), 128)
            g = mode_forces(modes_of(cell, r, l), mod_ext[cell, r, l])
            for q in range(4):
                for c in range(3):
                    if cell >= 1:
                        value = g[(q, c)] - g[(4 + q, c)] if q else -g[(4 + q, c)]
                        if cell == xc:
                            value = value + out[q, c, cell - 1, r, l] if xc > 1 else value
                        elif cell > 1:
                            value = value + out[q, c, cell - 1, r, l]
                        out[q, c, cell - 1, r, l] = value
                    if cell + 1 <= xc:
                        value = g[(q, c)] + g[(4 + q, c)] if q else g[(4 + q, c)]
                        if cell == 0:
                            value = value + out[q, c, cell, r, l]
                        out[q, c, cell, r, l] = value
            return carry

        lax.fori_loop(0, rows // 8 * lanes, body, 0)

    def next_plane(level, x):
        u, v = levels[level], levels[level + 1]
        for c in range(3):
            part = lambda q, start: out[q, c, x - 1, start : start + yc]
            even = (part(0, 0) + part(2, 0)) + (part(0, 1) - part(2, 1))
            odd = (part(1, 0) + part(3, 0)) + (part(1, 1) - part(3, 1))
            image = (even + odd) + above(even - odd)
            value = u[c, x, base : base + yc]
            weighted = image - SHIFT * (diag[x - 1] * value)
            following = inv[x - 1] * weighted
            v[c, x, base : base + yc] = following
            set_edges(level + 1, x, c, following)
            sums[2 * level + 1] += folded(value * weighted)
            sums[2 * level + 2] += folded(following * weighted)

    for level in range(2):
        u = levels[level]
        from_y.wait_recv()
        for x in range(1, xc + 1):
            fill_edges(level, x)
            split_modes(u, x, -1, rows)
        for cell in range(1, xc):
            apply_cell(cell)
        for copy in from_next:
            copy.wait_recv()
        fill_edges(level, xc + 1)
        split_modes(u, xc + 1, -1, rows)
        apply_cell(xc)
        for x in range(xc, 1, -1):
            next_plane(level, x)
        if level == 0:
            later_prev = send_next(1)
        for copy in from_prev:
            copy.wait_recv()
        fill_edges(level, 0)
        split_modes(u, 0, -1, rows)
        apply_cell(0)
        next_plane(level, 1)
        from_next = send_prev(level + 1)
        from_y = send_y(level + 1)
        if level == 0:
            from_prev = later_prev

    def energies(cell, put):
        def body(t, carry):
            r = pl.ds(pl.multiple_of(t // lanes * 8, 8), 8)
            l = pl.ds(pl.multiple_of(lax.rem(t, lanes) * 128, 128), 128)
            put(r, l, mod_own[cell - 1, r, l] * mode_energy(modes_of(cell, r, l)))
            return carry

        lax.fori_loop(0, yc // 8 * lanes, body, 0)

    def add_energy(r, l, value):
        sums[5] += value

    from_y.wait_recv()
    for x in range(1, xc + 1):
        fill_edges(2, x)
        split_modes(u2, x, 0, yc)
    for cell in range(1, xc):
        energies(cell, add_energy)
    for copy in from_next:
        copy.wait_recv()
    fill_edges(2, xc + 1)
    split_modes(u2, xc + 1, 0, yc)
    energies(xc, add_energy)

    tile[...] = jnp.sum(sums[...], axis=1)
    copies = []
    for index, peer in enumerate(peers):
        copy = pltpu.make_async_remote_copy(
            src_ref=tile, dst_ref=tiles.at[index],
            send_sem=tile_send.at[index], recv_sem=tile_recv.at[index],
            device_id=peer, device_id_type=MESH,
        )
        copy.start()
        copies.append(copy)
    total = tile[...]
    for index, copy in enumerate(copies):
        copy.wait_recv()
        total = total + tiles[index]
    total = jnp.sum(total, axis=1, keepdims=True)
    h = [total[k : k + 1] for k in range(6)]
    h[5] = h[5] - SHIFT * h[4]

    def inner(first, second, shifted):
        result = None
        for i, a in enumerate(first):
            for j, b in enumerate(second):
                moment = h[i + j + 1] + SHIFT * h[i + j] if shifted else h[i + j]
                term = a * b * moment
                result = term if result is None else result + term
        return result

    one = jnp.ones_like(h[0])
    precond, direction = [one], [one]
    weights = [jnp.zeros_like(one)] * 3
    norm_now = h[0]
    for step in range(3):
        alpha = norm_now / inner(direction, direction, True)
        for i, d in enumerate(direction):
            weights[i] = weights[i] + alpha * d
        if step < 2:
            image = [SHIFT * d for d in direction] + [jnp.zeros_like(one)]
            for i, d in enumerate(direction):
                image[i + 1] = image[i + 1] + d
            precond = precond + [jnp.zeros_like(one)] * (len(image) - len(precond))
            precond = [p - alpha * q for p, q in zip(precond, image)]
            norm_next = inner(precond, precond, False)
            beta = norm_next / norm_now
            longer = direction + [jnp.zeros_like(one)]
            direction = [p + beta * d for p, d in zip(precond, longer)]
            norm_now = norm_next

    for copy in sent:
        copy.wait_send()
    for copy in copies:
        copy.wait_send()
    for x in range(1, xc + 2):
        for c in range(3):
            where = (c, x, slice(base, base + yc + 8))
            value = weights[0] * u0[where] + weights[1] * u1[where] + weights[2] * u2[where]
            u0[where] = value
            if x <= xc:
                disp_out[c, x - 1] = value[0:yc]
        split_modes(u0, x, 0, yc)

    for cell in range(1, xc + 1):
        def put(r, l, value, cell=cell):
            sens_out[cell - 1, r, l] = -value

        energies(cell, put)


def per_device(n_gx, body_force, phase_label, grain_modulus):
    xc, yc, zc = phase_label.shape
    peers = 2 * n_gx - 1
    f32 = jnp.float32
    vmem = pltpu.VMEM
    ext = vmem((3, xc + 2, yc + 16, zc), f32)
    return pl.pallas_call(
        functools.partial(kernel, n_gx, xc, yc, zc),
        out_shape=(
            jax.ShapeDtypeStruct(body_force.shape, f32),
            jax.ShapeDtypeStruct(phase_label.shape, f32),
        ),
        in_specs=[pl.BlockSpec(memory_space=pltpu.VMEM)] * 3,
        out_specs=(pl.BlockSpec(memory_space=pltpu.VMEM),) * 2,
        scratch_shapes=[
            ext, ext, ext,
            vmem((3, xc, 8, zc), f32),
            vmem((3, xc + 2, 8, zc), f32),
            vmem((xc, yc, zc), f32),
            vmem((yc, zc), f32),
            vmem((xc, 8, zc), f32),
            vmem((xc + 1, 8, zc), f32),
            vmem((xc + 1, yc + 8, zc), f32),
            vmem((xc, yc, zc), f32),
            vmem((xc, yc, zc), f32),
            vmem((4, 3, xc + 2, yc + 8, zc), f32),
            vmem((4, 3, xc, yc + 8, zc), f32),
            vmem((8, 8, 128), f32),
            vmem((8, 128), f32),
            vmem((peers, 8, 128), f32),
            pltpu.SemaphoreType.DMA((16,)),
            pltpu.SemaphoreType.DMA((16,)),
            pltpu.SemaphoreType.DMA((peers,)),
            pltpu.SemaphoreType.DMA((peers,)),
        ],
        compiler_params=pltpu.CompilerParams(
            collective_id=0, has_side_effects=True, vmem_limit_bytes=40 * 1024 * 1024
        ),
        cost_estimate=pl.CostEstimate(
            flops=600 * xc * yc * zc, bytes_accessed=40 * xc * yc * zc, transcendentals=0
        ),
    )(body_force, phase_label, grain_modulus)


def solution(mesh):
    in_specs = (
        P(None, ("group", "gx"), "gy", None),
        P(("group", "gx"), "gy", None),
        P(("group", "gx"), "gy", None),
    )
    out_specs = (P(None, ("group", "gx"), "gy", None), P(("group", "gx"), "gy", None))
    return jax.shard_map(
        functools.partial(per_device, mesh.shape["gx"]),
        mesh=mesh, in_specs=in_specs, out_specs=out_specs, check_vma=False,
    )
```

time: 327 us -> 53 us (0.16)
  blocking collectives: 152 us -> 0 us
  waiting for transfers between devices: 71.8 us -> 0 us
  local copies, waits for them, and re-layouts: 54.4 us -> 4.2 us
  Pallas kernels: 0 us -> 47.9 us
  matrix products: 20.6 us -> 0 us
  other arithmetic: 12.2 us -> 0 us
  between operations: 8.22 us -> 0.65 us
  starting transfers between devices: 6.39 us -> 0 us
    psum x5 -> x0, blocking collectives: 152 us -> none  [the longest x3 91.8 us: inner_sum(): return lax.psum(jnp.sum(first * second), ('gx', 'gy'))]
    ppermute x16 -> x0, waiting for transfers between devices: 71.8 us -> none  [passed_along(): return lax.ppermute(value, axis, pairs)]
    pallas_call x0 -> x1, Pallas kernels: none -> 47.9 us  [per_device(): pl.pallas_call(functools.partial(kernel, n_gx, xc, yc, zc), out_shape=(ja...]
    dot_general x4 -> x0, matrix products: 20.6 us -> none  [element_forces(): jnp.dot(stiffness, corners, precision=lax.Precision.HIGHEST, preferred_el...]
    unnamed x62 -> x8, local copies, waits for them, and re-layouts: 24.5 us -> 4.2 us
    reshape x4 -> x0, local copies, waits for them, and re-layouts: 18.5 us -> none  [take_corners(): return jnp.stack(gathered, 0).reshape(24, -1)]
    ppermute x16 -> x0, starting transfers between devices: 6.39 us -> none  [passed_along(): return lax.ppermute(value, axis, pairs)]
    slice x32 -> x0, local copies, waits for them, and re-layouts: 5.92 us -> none  [the longest x4 2.83 us: spread_forces(): block = blocks[corner]]
  transfers between devices with their start and end apart: 16 -> 0, of which waited for: 12 -> 0; matrix products, arithmetic and copies ran while one was open for 2% -> 0% of each run, Pallas kernels for 0% -> 0%
where the time goes in v1:
time: 53 us; the launch traced here: 52.8 us
  Pallas kernels  47.9 us (90%)
  local copies, waits for them, and re-layouts  4.2 us (8%)
  between operations  0.65 us (1%)
    pallas_call x1, Pallas kernels, per_device(): pl.pallas_call(functools.partial(kernel, n_gx, xc, yc, zc), out_shape=(ja...  47.9 us
    unnamed x8, local copies, waits for them, and re-layouts  4.2 us

profile of v1, /device:TPU:0, one launch (start us, length us, event | category | flops | bytes accessed | tf_op | source)
XLA Modules:
  0.0 52.8 jit_solution(14942796863122777834)
XLA Ops:
  0.6 0.0 copy-start
  0.6 1.0 %copy-done = f32[3,2,32,512]{3,2,1,0:T(8,128)S(1)} copy-done((f32[3,2,32,512]{3,2,1,0:T(8,128)S(1)}, f32[3,2,32,512]{3,2,1,0:T(8,128)}, u32[]{:S(2)}) %copy-start) | copy-done | bytes 393240
  1.6 0.0 copy-start.1
  1.6 0.9 %copy-done.1 = s32[2,32,512]{2,1,0:T(8,128)S(1)} copy-done((s32[2,32,512]{2,1,0:T(8,128)S(1)}, s32[2,32,512]{2,1,0:T(8,128)}, u32[]{:S(2)}) %copy-start.1) | copy-done | bytes 131096
  2.5 0.0 copy-start.2
  2.5 0.9 %copy-done.2 = f32[2,32,512]{2,1,0:T(8,128)S(1)} copy-done((f32[2,32,512]{2,1,0:T(8,128)S(1)}, f32[2,32,512]{2,1,0:T(8,128)}, u32[]{:S(2)}) %copy-start.2) | copy-done | bytes 131096
  3.4 47.9 %shard_map.50 = (f32[3,2,32,512]{3,2,1,0:T(8,128)S(1)}, f32[2,32,512]{2,1,0:T(8,128)S(1)}) custom-call(f32[3,2,32,512]{3,2,1,0:T(8,128)S(1)} %copy-done, s32[2,32,512]{2,1,0:T(8,128)S(1)} %copy-done.1, f32[2,32,512]{2,1,0:T(8,128)S(1)} %copy-done.2), custom_call_target="tpu_custom_call" | custom-call | flops 19660800 | bytes 1310720 | tf_op jit(solution)/shard_map/pallas_call | solution.py:449
  51.4 0.7 %copy.7 = f32[3,2,32,512]{3,2,1,0:T(8,128)} copy(f32[3,2,32,512]{3,2,1,0:T(8,128)S(1)} %get-tuple-element.4) | data formatting | bytes 786432
  52.1 0.7 %copy.8 = f32[2,32,512]{2,1,0:T(8,128)} copy(f32[2,32,512]{2,1,0:T(8,128)S(1)} %get-tuple-element.5) | data formatting | bytes 262144
Async XLA Ops:
  0.6 1.0 %copy-start = (f32[3,2,32,512]{3,2,1,0:T(8,128)S(1)}, f32[3,2,32,512]{3,2,1,0:T(8,128)}, u32[]{:S(2)}) copy-start(f32[3,2,32,512]{3,2,1,0:T(8,128)} %force.1) | copy-start | bytes 1179652
  1.6 0.9 %copy-start.1 = (s32[2,32,512]{2,1,0:T(8,128)S(1)}, s32[2,32,512]{2,1,0:T(8,128)}, u32[]{:S(2)}) copy-start(s32[2,32,512]{2,1,0:T(8,128)} %label.1) | copy-start | bytes 393220
  2.5 0.9 %copy-start.2 = (f32[2,32,512]{2,1,0:T(8,128)S(1)}, f32[2,32,512]{2,1,0:T(8,128)}, u32[]{:S(2)}) copy-start(f32[2,32,512]{2,1,0:T(8,128)} %grain.1) | copy-start | bytes 393220

commit v2 on v1

--- a/solution.py
+++ b/solution.py
@@ -130,7 +130,8 @@
 
 def kernel(
     n_gx, xc, yc, zc,
-    force, label, grain, disp_out, sens_out,
+    force_in, label_in, grain_in, disp_out, sens_out,
+    force, label, grain, in_sem,
     u0, u1, u2, edge_out, edge_in, mod_own, mod_halo, mod_edge_out, mod_edge_in,
     mod_ext, diag, inv, yz, out, sums, tile, tiles, send_sem, recv_sem, tile_send, tile_recv,
 ):
@@ -149,6 +150,11 @@
                     "gy": other if flip else gy,
                 })
 
+    loads = []
+    for index, (src, dst) in enumerate(((label_in, label), (grain_in, grain), (force_in, force))):
+        load = pltpu.make_async_copy(src, dst, in_sem.at[index])
+        load.start()
+        loads.append(load)
     barrier = pltpu.get_barrier_semaphore()
     for peer in peers:
         pl.semaphore_signal(barrier, inc=1, device_id=peer, device_id_type=MESH)
@@ -173,11 +179,6 @@
         sent.append(copy)
         return copy
 
-    for x in range(xc):
-        values = jnp.where(label[x] == 1, grain[x], jnp.float32(PORE))
-        mod_own[x] = values
-        mod_edge_out[x, 0:1] = values[yc - 1 : yc]
-        mod_ext[x + 1, 1 : yc + 1] = values
     for x in range(xc + 1):
         mod_ext[x, yc + 1 : rows] = jnp.zeros((rows - yc - 1, zc), jnp.float32)
     for u in levels:
@@ -190,6 +191,13 @@
             edge_out[level, x, 6:8] = jnp.zeros((2, zc), jnp.float32)
     sums[...] = jnp.zeros_like(sums)
 
+    loads[0].wait()
+    loads[1].wait()
+    for x in range(xc):
+        values = jnp.where(label[x] == 1, grain[x], jnp.float32(PORE))
+        mod_own[x] = values
+        mod_edge_out[x, 0:1] = values[yc - 1 : yc]
+        mod_ext[x + 1, 1 : yc + 1] = values
     pl.semaphore_wait(barrier, len(peers))
     mod_y = send(mod_edge_out, mod_edge_in.at[pl.ds(1, xc)], gx, other)
     mod_x = send(mod_own.at[xc - 1], mod_halo, nxt, gy)
@@ -212,26 +220,34 @@
     def send_y(level):
         return send(edge_out.at[level], edge_in.at[level, pl.ds(1, xc)], gx, other)
 
-    def send_next(level):
+    def face_next(level, c):
         u = levels[level]
-        return (
-            send(u.at[:, xc, own], u.at[:, 0, own], nxt, gy),
-            send(edge_out.at[level, xc - 1], edge_in.at[level, 0], nxt, other),
-        )
-
-    def send_prev(level):
+        return send(u.at[c, xc, own], u.at[c, 0, own], nxt, gy)
+
+    def face_prev(level, c):
         u = levels[level]
-        return (
-            send(u.at[:, 1, own], u.at[:, xc + 1, own], prv, gy),
-            send(edge_out.at[level, 0], edge_in.at[level, xc + 1], prv, other),
-        )
+        return send(u.at[c, 1, own], u.at[c, xc + 1, own], prv, gy)
+
+    def rows_next(level):
+        return send(edge_out.at[level, xc - 1], edge_in.at[level, 0], nxt, other)
+
+    def rows_prev(level):
+        return send(edge_out.at[level, 0], edge_in.at[level, xc + 1], prv, other)
 
     def fill_edges(level, x):
         for c in range(3):
             levels[level][c, x, base + yc : base + yc + 1] = edge_in[level, x, c : c + 1]
             levels[level][c, x, base - 1 : base] = edge_in[level, x, 3 + c : 4 + c]
 
-    def start_plane(x):
+    from_prev, from_next = [[], [], []], [[], [], []]
+
+    def faces(x, level, c):
+        if x == xc and level < 2:
+            from_prev[level].append(face_next(level, c))
+        if x == 1:
+            from_next[level].append(face_prev(level, c))
+
+    def start_plane(x, faces):
         total = mod_ext[x - 1, 0:yc] + mod_ext[x - 1, 1 : yc + 1]
         total = total + mod_ext[x, 0:yc] + mod_ext[x, 1 : yc + 1]
         total = (total + above(total)) * K0_DIAGONAL
@@ -243,20 +259,25 @@
             value = inverse * load
             u0[c, x, base : base + yc] = value
             set_edges(0, x, c, value)
+            faces(x, 0, c)
             sums[0] += folded(value * load)
 
+    loads[2].wait()
     mod_y.wait_recv()
     for x in range(1, xc + 1):
         mod_ext[x, 0:1] = mod_edge_in[x, 0:1]
     for x in range(xc, 1, -1):
-        start_plane(x)
-    from_prev = send_next(0)
+        start_plane(x, faces)
+        if x == xc:
+            from_prev[0].append(rows_next(0))
     mod_x.wait_recv()
     mod_xy.wait_recv()
     mod_ext[0, 0:1] = mod_edge_in[0, 0:1]
     mod_ext[0, 1 : yc + 1] = mod_halo[...]
-    start_plane(1)
-    from_next = send_prev(0)
+    start_plane(1, faces)
+    if xc == 1:
+        from_prev[0].append(rows_next(0))
+    from_next[0].append(rows_prev(0))
     from_y = send_y(0)
 
     def split_modes(u, x, first, count):
@@ -318,6 +339,7 @@
             following = inv[x - 1] * weighted
             v[c, x, base : base + yc] = following
             set_edges(level + 1, x, c, following)
+            faces(x, level + 1, c)
             sums[2 * level + 1] += folded(value * weighted)
             sums[2 * level + 2] += folded(following * weighted)
 
@@ -329,25 +351,25 @@
             split_modes(u, x, -1, rows)
         for cell in range(1, xc):
             apply_cell(cell)
-        for copy in from_next:
+        for copy in from_next[level]:
             copy.wait_recv()
         fill_edges(level, xc + 1)
         split_modes(u, xc + 1, -1, rows)
         apply_cell(xc)
         for x in range(xc, 1, -1):
             next_plane(level, x)
-        if level == 0:
-            later_prev = send_next(1)
-        for copy in from_prev:
+            if x == xc and level == 0:
+                from_prev[1].append(rows_next(1))
+        for copy in from_prev[level]:
             copy.wait_recv()
         fill_edges(level, 0)
         split_modes(u, 0, -1, rows)
         apply_cell(0)
         next_plane(level, 1)
-        from_next = send_prev(level + 1)
+        if xc == 1 and level == 0:
+            from_prev[1].append(rows_next(1))
+        from_next[level + 1].append(rows_prev(level + 1))
         from_y = send_y(level + 1)
-        if level == 0:
-            from_prev = later_prev
 
     def energies(cell, put):
         def body(t, carry):
@@ -367,7 +389,7 @@
         split_modes(u2, x, 0, yc)
     for cell in range(1, xc):
         energies(cell, add_energy)
-    for copy in from_next:
+    for copy in from_next[2]:
         copy.wait_recv()
     fill_edges(2, xc + 1)
     split_modes(u2, xc + 1, 0, yc)
@@ -452,9 +474,13 @@
             jax.ShapeDtypeStruct(body_force.shape, f32),
             jax.ShapeDtypeStruct(phase_label.shape, f32),
         ),
-        in_specs=[pl.BlockSpec(memory_space=pltpu.VMEM)] * 3,
+        in_specs=[pl.BlockSpec(memory_space=pl.ANY)] * 3,
         out_specs=(pl.BlockSpec(memory_space=pltpu.VMEM),) * 2,
         scratch_shapes=[
+            vmem((3, xc, yc, zc), f32),
+            vmem((xc, yc, zc), jnp.int32),
+            vmem((xc, yc, zc), f32),
+            pltpu.SemaphoreType.DMA((3,)),
             ext, ext, ext,
             vmem((3, xc, 8, zc), f32),
             vmem((3, xc + 2, 8, zc), f32),
@@ -470,13 +496,13 @@
             vmem((8, 8, 128), f32),
             vmem((8, 128), f32),
             vmem((peers, 8, 128), f32),
-            pltpu.SemaphoreType.DMA((16,)),
-            pltpu.SemaphoreType.DMA((16,)),
+            pltpu.SemaphoreType.DMA((32,)),
+            pltpu.SemaphoreType.DMA((32,)),
             pltpu.SemaphoreType.DMA((peers,)),
             pltpu.SemaphoreType.DMA((peers,)),
         ],
         compiler_params=pltpu.CompilerParams(
-            collective_id=0, has_side_effects=True, vmem_limit_bytes=40 * 1024 * 1024
+            collective_id=0, has_side_effects=True, vmem_limit_bytes=60 * 1024 * 1024
         ),
         cost_estimate=pl.CostEstimate(
             flops=600 * xc * yc * zc, bytes_accessed=40 * xc * yc * zc, transcendentals=0

time: 53 us -> 52.2 us (0.985)
  local copies, waits for them, and re-layouts: 4.2 us -> 2.47 us
  Pallas kernels: 47.9 us -> 48.9 us
    unnamed x8 -> x4, local copies, waits for them, and re-layouts: 4.2 us -> 2.47 us
    pallas_call x1, Pallas kernels: 47.9 us -> 48.9 us  [per_device(): pl.pallas_call(functools.partial(kernel, n_gx, xc, yc, zc), out_shape=(ja...]
where the time goes in v2:
time: 52.2 us; the launch traced here: 52 us
  Pallas kernels  48.9 us (94%)
  local copies, waits for them, and re-layouts  2.47 us (5%)
  between operations  0.65 us (1%)
    pallas_call x1, Pallas kernels, per_device(): pl.pallas_call(functools.partial(kernel, n_gx, xc, yc, zc), out_shape=(ja...  48.9 us
    unnamed x4, local copies, waits for them, and re-layouts  2.47 us

profile of v2, /device:TPU:0, one launch (start us, length us, event | category | flops | bytes accessed | tf_op | source)
XLA Modules:
  0.0 52.0 jit_solution(12733625932624278096)
XLA Ops:
  0.6 48.9 %shard_map.50 = (f32[3,2,32,512]{3,2,1,0:T(8,128)}, f32[2,32,512]{2,1,0:T(8,128)}) custom-call(f32[3,2,32,512]{3,2,1,0:T(8,128)} %force_in.1, s32[2,32,512]{2,1,0:T(8,128)} %label_in.1, f32[2,32,512]{2,1,0:T(8,128)} %grain_in.1), custom_call_target="tpu_custom_call" | custom-call | flops 19660800 | bytes 1310720 | tf_op jit(solution)/shard_map/pallas_call | solution.py:471
  49.6 0.0 copy-start
  49.6 1.8 %copy.7 = f32[3,2,32,512]{3,2,1,0:T(8,128)} copy(f32[3,2,32,512]{3,2,1,0:T(8,128)} %get-tuple-element.4) | data formatting | bytes 786432
  51.4 0.0 copy-done
  51.4 0.7 %copy.8 = f32[2,32,512]{2,1,0:T(8,128)} copy(f32[2,32,512]{2,1,0:T(8,128)S(1)} %copy-done) | data formatting | bytes 262144
Async XLA Ops:
  49.6 1.8 %copy-start = (f32[2,32,512]{2,1,0:T(8,128)S(1)}, f32[2,32,512]{2,1,0:T(8,128)}, u32[]{:S(2)}) copy-start(f32[2,32,512]{2,1,0:T(8,128)} %get-tuple-element.5) | copy-start | bytes 393220

commit v3 on v2

--- a/solution.py
+++ b/solution.py
@@ -131,7 +131,7 @@
 def kernel(
     n_gx, xc, yc, zc,
     force_in, label_in, grain_in, disp_out, sens_out,
-    force, label, grain, in_sem,
+    force, label, grain, in_sem, final, sens, out_sem,
     u0, u1, u2, edge_out, edge_in, mod_own, mod_halo, mod_edge_out, mod_edge_in,
     mod_ext, diag, inv, yz, out, sums, tile, tiles, send_sem, recv_sem, tile_send, tile_recv,
 ):
@@ -442,24 +442,31 @@
             direction = [p + beta * d for p, d in zip(precond, longer)]
             norm_now = norm_next
 
-    for copy in sent:
-        copy.wait_send()
-    for copy in copies:
-        copy.wait_send()
+    stores = []
     for x in range(1, xc + 2):
         for c in range(3):
             where = (c, x, slice(base, base + yc + 8))
             value = weights[0] * u0[where] + weights[1] * u1[where] + weights[2] * u2[where]
-            u0[where] = value
-            if x <= xc:
-                disp_out[c, x - 1] = value[0:yc]
-        split_modes(u0, x, 0, yc)
+            final[where] = value
+        if x <= xc:
+            copy = pltpu.make_async_copy(final.at[:, x, own], disp_out.at[:, x - 1], out_sem.at[x - 1])
+            copy.start()
+            stores.append(copy)
+        split_modes(final, x, 0, yc)
 
     for cell in range(1, xc + 1):
         def put(r, l, value, cell=cell):
-            sens_out[cell - 1, r, l] = -value
+            sens[cell - 1, r, l] = -value
 
         energies(cell, put)
+        copy = pltpu.make_async_copy(sens.at[cell - 1], sens_out.at[cell - 1], out_sem.at[xc + cell - 1])
+        copy.start()
+        stores.append(copy)
+
+    for copy in sent + copies:
+        copy.wait_send()
+    for copy in stores:
+        copy.wait()
 
 
 def per_device(n_gx, body_force, phase_label, grain_modulus):
@@ -475,12 +482,15 @@
             jax.ShapeDtypeStruct(phase_label.shape, f32),
         ),
         in_specs=[pl.BlockSpec(memory_space=pl.ANY)] * 3,
-        out_specs=(pl.BlockSpec(memory_space=pltpu.VMEM),) * 2,
+        out_specs=(pl.BlockSpec(memory_space=pl.ANY),) * 2,
         scratch_shapes=[
             vmem((3, xc, yc, zc), f32),
             vmem((xc, yc, zc), jnp.int32),
             vmem((xc, yc, zc), f32),
             pltpu.SemaphoreType.DMA((3,)),
+            ext,
+            vmem((xc, yc, zc), f32),
+            pltpu.SemaphoreType.DMA((2 * xc,)),
             ext, ext, ext,
             vmem((3, xc, 8, zc), f32),
             vmem((3, xc + 2, 8, zc), f32),

time: 52.2 us -> 52 us (level)
  no operation moved by 1% of the time
where the time goes in v3:
time: 52 us; the launch traced here: 51.8 us
  Pallas kernels  48.7 us (94%)
  local copies, waits for them, and re-layouts  2.47 us (5%)
  between operations  0.65 us (1%)
    pallas_call x1, Pallas kernels, per_device(): pl.pallas_call(functools.partial(kernel, n_gx, xc, yc, zc), out_shape=(ja...  48.7 us
    unnamed x4, local copies, waits for them, and re-layouts  2.47 us

profile of v3, /device:TPU:0, one launch (start us, length us, event | category | flops | bytes accessed | tf_op | source)
XLA Modules:
  0.0 51.8 jit_solution(3216799417920525299)
XLA Ops:
  0.6 48.7 %shard_map.50 = (f32[3,2,32,512]{3,2,1,0:T(8,128)}, f32[2,32,512]{2,1,0:T(8,128)}) custom-call(f32[3,2,32,512]{3,2,1,0:T(8,128)} %force_in.1, s32[2,32,512]{2,1,0:T(8,128)} %label_in.1, f32[2,32,512]{2,1,0:T(8,128)} %grain_in.1), custom_call_target="tpu_custom_call" | custom-call | flops 19660800 | bytes 1310720 | tf_op jit(solution)/shard_map/pallas_call | solution.py:478
  49.3 0.0 copy-start
  49.3 1.8 %copy.7 = f32[3,2,32,512]{3,2,1,0:T(8,128)} copy(f32[3,2,32,512]{3,2,1,0:T(8,128)} %get-tuple-element.4) | data formatting | bytes 786432
  51.2 0.0 copy-done
  51.2 0.7 %copy.8 = f32[2,32,512]{2,1,0:T(8,128)} copy(f32[2,32,512]{2,1,0:T(8,128)S(1)} %copy-done) | data formatting | bytes 262144
Async XLA Ops:
  49.3 1.8 %copy-start = (f32[2,32,512]{2,1,0:T(8,128)S(1)}, f32[2,32,512]{2,1,0:T(8,128)}, u32[]{:S(2)}) copy-start(f32[2,32,512]{2,1,0:T(8,128)} %get-tuple-element.5) | copy-start | bytes 393220
